TPU v7x, 256 devices: a whole 4x4x8 slice. The times are simulated.
256 devices in a mesh: ctx: 128 (over y, x, z_lo, core), tp: 2 (over z_hi).
Axes of the slice: x: 4, y: 4, z: 8 (z_hi: 2, z_lo: 4; z = z_hi * 4 + z_lo), core: 2. Of those that a mesh axis runs over, the one named last changes fastest.
Arguments:
- query_proj: bfloat16 [16384, 4096], P('ctx', 'tp'), may hold values from -6 to 6
- key_proj: bfloat16 [16384, 4096], P('ctx', 'tp'), may hold values from -6 to 6
- value_proj: bfloat16 [16384, 4096], P('ctx', 'tp'), may hold values from -6 to 6
- out_grad: bfloat16 [16384, 4096], P('ctx', 'tp'), may hold values from -6 to 6
- raw_filter: bfloat16 [16384, 2048], P('ctx'), may hold values from -6 to 6
Outputs:
- query_grad: bfloat16 [16384, 4096], P('ctx', 'tp')
- key_grad: bfloat16 [16384, 4096], P('ctx', 'tp')
- value_grad: bfloat16 [16384, 4096], P('ctx', 'tp')
- filter_grad: bfloat16 [16384, 2048], P('ctx')
All inputs are finite; a program needn't handle non-finite values.
Results may differ from a plain program's by a relative error of at most 0.0057.
Values may be sent and summed in bfloat16 or wider, within the bound.
A program may use at most 128 MiB of HBM per device.

v0:
```python
import functools
import math

import jax
import jax.numpy as jnp
import ml_dtypes
import numpy as np
from jax import lax
from jax.experimental import pallas as pl
from jax.experimental.pallas import tpu as pltpu
from jax.sharding import PartitionSpec as P

MESH = pl.DeviceIdType.MESH
BF16 = jnp.bfloat16
F32 = jnp.float32

BLOCK = 128
LONG = 256
PERIOD = BLOCK * LONG
COLS = 16
DEPTH = 16
OWN = 8


def split_table(table):
    high = table.astype(ml_dtypes.bfloat16)
    low = (table - high.astype(np.float64)).astype(ml_dtypes.bfloat16)
    return high, low


def tables():
    freq = np.arange(LONG)[:, None]
    block = np.arange(BLOCK)[None, :]
    long_angle = 2.0 * math.pi * ((freq * block) % LONG) / LONG
    cos_long, sin_long = np.cos(long_angle), np.sin(long_angle)
    outer = np.block([[cos_long, sin_long], [-sin_long, cos_long]])
    small_angle = 2.0 * math.pi * ((block.T * block) % BLOCK) / BLOCK
    cos_small, sin_small = np.cos(small_angle), np.sin(small_angle)
    inner = np.block([[cos_small, -sin_small], [sin_small, cos_small]])
    twid_angle = 2.0 * math.pi * (freq * block) / PERIOD
    twid_cos = np.cos(twid_angle).astype(np.float32)
    twid_sin = np.sin(twid_angle).astype(np.float32)
    return (
        *split_table(outer),
        *split_table(inner),
        *split_table(inner.T),
        *split_table(outer.T),
        twid_cos,
        twid_sin,
    )


def mul(left, right):
    return jnp.dot(left, right, preferred_element_type=F32)


def halves(value):
    high = value.astype(BF16)
    return high, (value - high.astype(F32)).astype(BF16)


def kernel(
    q_ref, k_ref, v_ref, g_ref, f_ref,
    out_hi, out_lo, in_hi, in_lo, back_hi, back_lo, last_hi, last_lo, cos_ref, sin_ref,
    dq_ref, dk_ref, dv_ref, df_ref,
    cut_f, cut_p, cut_g, mid_f, mid_p, mid_g, got_f, got_p, got_g,
    send_c, send_d, send_l, half_c, half_d, half_l, end_c, end_d, end_l,
    wide, spec_h, spec_p,
    z_send, z_recv, xy_send, xy_recv, loc,
):
    ctx, tp = lax.axis_index("ctx"), lax.axis_index("tp")
    col = ctx // 8
    low = ctx % 8
    zc = tp * 8 + low
    z, core = zc // 2, zc % 2

    def in_column(index):
        return (col * 8 + index % 8, index // 8)

    def in_plane(index):
        return (index * 8 + low, tp)

    def around(step):
        return lax.rem(zc + step, DEPTH)

    def beside(step):
        across = lax.rem(col % 4 + step % 4, 4)
        along = lax.rem(col // 4 + step // 4, 4)
        return along * 4 + across

    barrier = pltpu.get_barrier_semaphore()

    def greet(step, carry):
        pl.semaphore_signal(barrier, inc=1, device_id=in_column(around(step)), device_id_type=MESH)
        pl.semaphore_signal(barrier, inc=1, device_id=in_plane(beside(step)), device_id_type=MESH)
        return carry

    lax.fori_loop(1, 16, greet, 0)

    def z_copy(kind, src, dst, index):
        return pltpu.make_async_remote_copy(
            src_ref=src, dst_ref=dst, send_sem=z_send.at[kind], recv_sem=z_recv.at[kind],
            device_id=in_column(index), device_id_type=MESH,
        )

    def xy_copy(kind, src, dst, index):
        return pltpu.make_async_remote_copy(
            src_ref=src, dst_ref=dst, send_sem=xy_send.at[kind], recv_sem=xy_recv.at[kind],
            device_id=in_plane(index), device_id_type=MESH,
        )

    def columns(index):
        return pl.ds(pl.multiple_of(index * BLOCK, BLOCK), BLOCK)

    def turned(block):
        return block.T.astype(BF16).reshape(COLS, OWN, BLOCK)

    def cut_filter(step, carry):
        index = around(step)
        cut_f[index] = turned(f_ref[:, columns(index)].astype(F32))
        return carry

    lax.fori_loop(0, DEPTH, cut_filter, 0)
    pl.semaphore_wait(barrier, 30)
    flip = lax.rem(col // 4 + col + core, 2)

    def send_filter(step, carry):
        turn = step // 2
        away = jnp.where(turn == 3, jnp.where(flip == 0, 2, 6), jnp.where(turn == 2, 7, turn))
        index = lax.rem(z + away, 8) * 2 + lax.rem(core + step, 2)
        z_copy(0, cut_f.at[index], mid_f.at[low], index).start()
        return carry

    lax.fori_loop(1, 8, send_filter, 0)
    own_f = pltpu.make_async_copy(cut_f.at[zc], mid_f.at[low], loc.at[0])
    own_f.start()

    def cut_product(kind, left, right, cut, mid):
        def one(step, carry):
            index = around(step)
            cols = columns(index)
            product = left[:, cols].astype(F32) * right[:, cols].astype(F32)
            cut[index] = turned(product.astype(BF16).astype(F32))
            z_copy(kind, cut.at[index], mid.at[zc], index).start()
            return carry

        lax.fori_loop(1, DEPTH, one, 0)
        cols = columns(zc)
        product = left[:, cols].astype(F32) * right[:, cols].astype(F32)
        mid[zc] = turned(product.astype(BF16).astype(F32))

    cut_product(1, q_ref, k_ref, cut_p, mid_p)
    cut_product(2, g_ref, v_ref, cut_g, mid_g)

    def z_done(kind, mid, count):
        part = mid.at[pl.ds(0, count)]
        z_copy(kind, part, part, around(1)).wait_recv()

    def cross(kind, mid, got):
        def one(step, carry):
            index = beside(step)
            xy_copy(kind, mid.at[:, index], got.at[col], index).start()
            return carry

        lax.fori_loop(1, COLS, one, 0)
        own = pltpu.make_async_copy(mid.at[:, col], got.at[col], loc.at[kind])
        own.start()
        return own

    def xy_done(kind, got, own):
        own.wait()
        part = got.at[pl.ds(0, COLS - 1)]
        xy_copy(kind, part, part, beside(1)).wait_recv()

    cos, sin = cos_ref[...], sin_ref[...]
    cos2 = jnp.concatenate([cos, cos], axis=1)
    sin2 = jnp.concatenate([sin, sin], axis=1)

    def forward(sig, depth):
        first = mul(out_hi[:, :depth], sig) + mul(out_lo[:, :depth], sig)
        real, imag = first[:LONG], first[LONG:]
        tr = real * cos2 + imag * sin2
        ti = imag * cos2 - real * sin2
        rows = jnp.concatenate(
            [
                jnp.concatenate([tr[:, :BLOCK], ti[:, :BLOCK]], axis=1),
                jnp.concatenate([tr[:, BLOCK:], ti[:, BLOCK:]], axis=1),
            ],
            axis=0,
        )
        hi, lo = halves(rows)
        return mul(hi, in_hi[...]) + mul(hi, in_lo[...]) + mul(lo, in_hi[...])

    def inverse(spec, rows):
        hi, lo = halves(spec)
        mixed = mul(hi, back_hi[...]) + mul(hi, back_lo[...]) + mul(lo, back_hi[...])
        real = jnp.concatenate([mixed[:LONG, :BLOCK], mixed[LONG:, :BLOCK]], axis=1)
        imag = jnp.concatenate([mixed[:LONG, BLOCK:], mixed[LONG:, BLOCK:]], axis=1)
        both = jnp.concatenate([real * cos2 - imag * sin2, real * sin2 + imag * cos2], axis=0)
        hi, lo = halves(both)
        total = (
            mul(last_hi[:rows], hi) + mul(last_lo[:rows], hi) + mul(last_hi[:rows], lo)
        )
        return total * (1.0 / PERIOD / BLOCK)

    def times(left, right, conjugate):
        lr, li = left[:, :BLOCK], left[:, BLOCK:]
        rr, ri = right[:, :BLOCK], right[:, BLOCK:]
        if conjugate:
            return jnp.concatenate([lr * rr + li * ri, lr * ri - li * rr], axis=1)
        return jnp.concatenate([lr * rr - li * ri, lr * ri + li * rr], axis=1)

    def load(base, jump):
        parts = [wide[pl.ds(base + n * jump, 8, stride=OWN), :] for n in range(COLS)]
        return jnp.concatenate(parts, axis=0).astype(BF16)

    def store(base, jump, value):
        for n in range(COLS):
            wide[pl.ds(base + n * jump, 8, stride=OWN), :] = value[n * 8 : n * 8 + 8]

    def load_pair(one):
        top = [load(one, BLOCK), load(one + 1, BLOCK)]
        bottom = [load(one + 64, BLOCK), load(one + 65, BLOCK)]
        return jnp.concatenate(
            [jnp.concatenate(top, axis=1), jnp.concatenate(bottom, axis=1)], axis=0
        )

    def store_pair(one, value):
        store(one, BLOCK, value[:BLOCK, :BLOCK])
        store(one + 1, BLOCK, value[:BLOCK, BLOCK:])
        store(one + 64, BLOCK, value[BLOCK:, :BLOCK])
        store(one + 65, BLOCK, value[BLOCK:, BLOCK:])

    def spread(got):
        rows = got.shape[0] * got.shape[1] * OWN
        wide[pl.ds(0, rows), :] = got[...].astype(F32).reshape(rows, BLOCK)

    def gather(out):
        rows = out.shape[0] * out.shape[1] * OWN
        out[...] = wide[pl.ds(0, rows), :].astype(BF16).reshape(out.shape)

    own_f.wait()
    z_done(0, mid_f, 7)
    side_f = cross(0, mid_f, got_f)
    xy_done(0, got_f, side_f)
    spread(got_f)

    def filter_spectrum(pair, carry):
        one = 2 * pair
        sig = jnp.concatenate([load(one, 64), load(one + 1, 64)], axis=1)
        spec_h[pair] = forward(sig, BLOCK)
        return carry

    lax.fori_loop(0, OWN // 2, filter_spectrum, 0)

    z_done(1, mid_p, DEPTH - 1)
    side_p = cross(1, mid_p, got_p)
    xy_done(1, got_p, side_p)
    spread(got_p)

    def convolve(pair, carry):
        spec = forward(load_pair(2 * pair), 2 * BLOCK)
        spec_p[pair] = spec
        store_pair(2 * pair, inverse(times(spec_h[pair], spec, False), 2 * BLOCK))
        return carry

    lax.fori_loop(0, OWN // 2, convolve, 0)
    gather(send_c)

    def deliver(kind, out, mid):
        def one(step, carry):
            index = around(step)
            where = lax.rem(index, out.shape[1])
            z_copy(kind, out.at[:, where], mid.at[zc], index).start()
            return carry

        lax.fori_loop(1, DEPTH, one, 0)
        own = pltpu.make_async_copy(out.at[:, lax.rem(zc, out.shape[1])], mid.at[zc], loc.at[kind + 3])
        own.start()
        return own

    z_done(2, mid_g, DEPTH - 1)
    side_g = cross(2, mid_g, got_g)
    own_c = deliver(3, send_c, half_c)

    xy_done(2, got_g, side_g)
    spread(got_g)

    def correlate(pair, carry):
        spec = forward(load_pair(2 * pair), 2 * BLOCK)
        store_pair(2 * pair, inverse(times(spec_h[pair], spec, True), 2 * BLOCK))
        spec_p[pair] = times(spec_p[pair], spec, True)
        return carry

    lax.fori_loop(0, OWN // 2, correlate, 0)
    gather(send_d)
    own_d = deliver(4, send_d, half_d)

    def lag(pair, carry):
        value = inverse(spec_p[pair], BLOCK)
        store(2 * pair, 64, value[:, :BLOCK])
        store(2 * pair + 1, 64, value[:, BLOCK:])
        return carry

    lax.fori_loop(0, OWN // 2, lag, 0)
    gather(send_l)
    own_l = deliver(5, send_l, half_l)

    own_c.wait()
    z_done(3, half_c, DEPTH - 1)
    side_c = cross(3, half_c, end_c)
    xy_done(3, end_c, side_c)

    def home(end, index):
        return end[:, index].astype(F32).reshape(BLOCK, BLOCK).T

    def finish_value(index, carry):
        cols = columns(index)
        dv_ref[:, cols] = (home(end_c, index) * g_ref[:, cols].astype(F32)).astype(BF16)
        return carry

    lax.fori_loop(0, DEPTH, finish_value, 0)

    own_d.wait()
    z_done(4, half_d, DEPTH - 1)
    side_d = cross(4, half_d, end_d)
    xy_done(4, end_d, side_d)

    def finish_gates(index, carry):
        cols = columns(index)
        back = home(end_d, index)
        dq_ref[:, cols] = (back * k_ref[:, cols].astype(F32)).astype(BF16)
        dk_ref[:, cols] = (back * q_ref[:, cols].astype(F32)).astype(BF16)
        return carry

    lax.fori_loop(0, DEPTH, finish_gates, 0)

    own_l.wait()
    z_done(5, half_l, DEPTH - 1)
    side_l = cross(5, half_l, end_l)
    xy_done(5, end_l, side_l)

    def finish_filter(index, carry):
        df_ref[:, columns(index)] = home(end_l, index).astype(BF16)
        return carry

    lax.fori_loop(0, DEPTH, finish_filter, 0)

    for kind in range(6):
        part = mid_f.at[pl.ds(0, 7)] if kind == 0 else mid_p.at[pl.ds(0, DEPTH - 1)]
        z_copy(kind, part, part, around(1)).wait_send()
        part = (got_f if kind == 0 else got_p).at[pl.ds(0, COLS - 1)]
        xy_copy(kind, part, part, beside(1)).wait_send()


def per_device(query_proj, key_proj, value_proj, out_grad, raw_filter):
    shape = jax.ShapeDtypeStruct(query_proj.shape, BF16)
    full = pltpu.VMEM((COLS, DEPTH, OWN, BLOCK), BF16)
    half = pltpu.VMEM((COLS, DEPTH // 2, OWN, BLOCK), BF16)
    near = pltpu.VMEM((DEPTH // 2, COLS, OWN, BLOCK), BF16)
    consts = tuple(jnp.asarray(table) for table in tables())
    vmem = pl.BlockSpec(memory_space=pltpu.VMEM)
    return pl.pallas_call(
        kernel,
        out_shape=(shape,) * 4,
        in_specs=[vmem] * (5 + len(consts)),
        out_specs=(vmem,) * 4,
        scratch_shapes=[
            full, full, full, near, full, full, half, full, full,
            full, full, half, full, full, full, full, full, full,
            pltpu.VMEM((COLS * DEPTH * OWN, BLOCK), F32),
            pltpu.VMEM((OWN // 2, 2 * LONG, 2 * BLOCK), F32),
            pltpu.VMEM((OWN // 2, 2 * LONG, 2 * BLOCK), F32),
            pltpu.SemaphoreType.DMA((6,)),
            pltpu.SemaphoreType.DMA((6,)),
            pltpu.SemaphoreType.DMA((6,)),
            pltpu.SemaphoreType.DMA((6,)),
            pltpu.SemaphoreType.DMA((9,)),
        ],
        compiler_params=pltpu.CompilerParams(
            collective_id=0, has_side_effects=True, vmem_limit_bytes=56 * 1024 * 1024
        ),
    )(query_proj, key_proj, value_proj, out_grad, raw_filter, *consts)


def solution(mesh):
    in_specs = (P("ctx", "tp"), P("ctx", "tp"), P("ctx", "tp"), P("ctx", "tp"), P("ctx", None))
    out_specs = (P("ctx", "tp"), P("ctx", "tp"), P("ctx", "tp"), P("ctx", None))
    return jax.shard_map(
        per_device, mesh=mesh, in_specs=in_specs, out_specs=out_specs, check_vma=False
    )
```

profile of v0, /device:TPU:1, one launch (start us, length us, event | category | flops | bytes accessed | tf_op | source)
XLA Modules:
  0.0 109.3 jit_solution(16734979772425792002)
XLA Ops:
  0.6 103.5 %shard_map.174 = (bf16[128,2048]{1,0:T(8,128)(2,1)}, bf16[128,2048]{1,0:T(8,128)(2,1)}, bf16[128,2048]{1,0:T(8,128)(2,1)}, bf16[128,2048]{1,0:T(8,128)(2,1)}) custom-call(bf16[128,2048]{1,0:T(8,128)(2,1)} %q_ref.1, bf16[128,2048]{1,0:T(8,128)(2,1)} %k_ref.1, bf16[128,2048]{1,0:T(8,128)(2,1)} %v_ref.1, bf16[128,2048]{1,0:T(8,128)(2,1)} %g_ref.1, ...), custom_call_target="tpu_custom_call" | custom-call | tf_op jit(solution)/shard_map/pallas_call | solution.py:363
  104.1 0.0 copy-start.2
  104.1 1.9 %copy.23 = bf16[128,2048]{1,0:T(8,128)(2,1)} copy(bf16[128,2048]{1,0:T(8,128)(2,1)} %get-tuple-element.8) | data formatting | bytes 1048576
  106.0 0.0 copy-done.2
  106.0 0.0 copy-start.1
  106.0 0.8 copy.24
  106.8 0.4 copy-done.1
  107.3 0.0 copy-start
  107.3 0.8 copy.25
  108.1 0.4 copy-done
  108.5 0.8 copy.26
Async XLA Ops:
  104.1 2.0 %copy-start.2 = (bf16[128,2048]{1,0:T(8,128)(2,1)S(1)}, bf16[128,2048]{1,0:T(8,128)(2,1)}, u32[]{:S(2)}) copy-start(bf16[128,2048]{1,0:T(8,128)(2,1)} %get-tuple-element.9) | copy-start | bytes 1572868
  106.0 1.2 %copy-start.1 = (bf16[128,2048]{1,0:T(8,128)(2,1)S(1)}, bf16[128,2048]{1,0:T(8,128)(2,1)}, u32[]{:S(2)}) copy-start(bf16[128,2048]{1,0:T(8,128)(2,1)} %get-tuple-element.10) | copy-start | bytes 1572868
  107.3 1.2 %copy-start = (bf16[128,2048]{1,0:T(8,128)(2,1)S(1)}, bf16[128,2048]{1,0:T(8,128)(2,1)}, u32[]{:S(2)}) copy-start(bf16[128,2048]{1,0:T(8,128)(2,1)} %get-tuple-element.11) | copy-start | bytes 1572868
where the time goes:
time: 110 us; the launch traced here: 109 us
  Pallas kernels  103 us (94%)
  local copies, waits for them, and re-layouts  5.19 us (5%)
    pallas_call x1, Pallas kernels, per_device(): pl.pallas_call(kernel, out_shape=(shape,) * 4, in_specs=[vmem] * (5 + len...  103 us
    unnamed x10, local copies, waits for them, and re-layouts  5.19 us

commit v1 on v0

v1 whole, which is shorter than its diff:
```python
import functools
import math

import jax
import jax.numpy as jnp
import ml_dtypes
import numpy as np
from jax import lax
from jax.experimental import pallas as pl
from jax.experimental.pallas import tpu as pltpu
from jax.sharding import PartitionSpec as P

MESH = pl.DeviceIdType.MESH
BF16 = jnp.bfloat16
F32 = jnp.float32

BLOCK = 128
LONG = 256
PERIOD = BLOCK * LONG
COLS = 16
DEPTH = 16
OWN = 8


def split_table(table):
    high = table.astype(ml_dtypes.bfloat16)
    low = (table - high.astype(np.float64)).astype(ml_dtypes.bfloat16)
    return np.stack([high, low])


def tables():
    freq = np.arange(LONG)[:, None]
    block = np.arange(BLOCK)[None, :]
    long_angle = 2.0 * math.pi * ((freq * block) % LONG) / LONG
    cos_long, sin_long = np.cos(long_angle), np.sin(long_angle)
    outer = np.block([[cos_long, sin_long], [-sin_long, cos_long]])
    small_angle = 2.0 * math.pi * ((block.T * block) % BLOCK) / BLOCK
    cos_small, sin_small = np.cos(small_angle), np.sin(small_angle)
    inner = np.block([[cos_small, -sin_small], [sin_small, cos_small]])
    twid_angle = 2.0 * math.pi * (freq * block) / PERIOD
    turn = np.stack([np.cos(twid_angle), np.sin(twid_angle)]).astype(np.float32)
    return (*(split_table(table) for table in (outer, inner, inner.T, outer.T)), turn)


def mul(left, right):
    return jnp.dot(left, right, preferred_element_type=F32)


def halves(value):
    high = value.astype(BF16)
    return high, (value - high.astype(F32)).astype(BF16)


def kernel(
    q_in, k_in, v_in, g_in, f_in, out_in, inn_in, back_in, last_in, turn_in,
    dq_out, dk_out, dv_out, df_out,
    q_ref, k_ref, v_ref, g_ref, f_ref, out_tab, inn_tab, back_tab, last_tab, turn_tab,
    dq_ref, dk_ref, dv_ref, df_ref,
    cut_f, mid_f, got_f, cut_p, got_p, cut_g, got_g,
    send_c, half_c, end_c, send_d, half_d, end_d, send_l, end_l,
    wide, spec_h, spec_p,
    z_send, z_recv, xy_send, xy_recv, far_send, far_recv, loc, fetch, leave, ready,
):
    ctx, tp = lax.axis_index("ctx"), lax.axis_index("tp")
    col = ctx // 8
    low = ctx % 8
    zc = tp * 8 + low
    z, core = zc // 2, zc % 2
    me = col * DEPTH + zc

    def device(there, depth):
        return (there * 8 + depth % 8, depth // 8)

    def around(step):
        return lax.rem(zc + step, DEPTH)

    def beside(step):
        across = lax.rem(col % 4 + step % 4, 4)
        along = lax.rem(col // 4 + step // 4, 4)
        return along * 4 + across

    depths = [around(step) for step in range(DEPTH)]
    barrier = pltpu.get_barrier_semaphore()

    def greet(step, carry):
        for target in (device(col, around(step)), device(beside(step), zc)):
            pl.semaphore_signal(barrier, inc=1, device_id=target, device_id_type=MESH)
        return carry

    lax.fori_loop(1, 16, greet, 0)

    arrivals = [
        pltpu.make_async_copy(src, dst, fetch.at[n])
        for n, (src, dst) in enumerate(
            (
                (f_in, f_ref), (q_in, q_ref), (k_in, k_ref), (g_in, g_ref), (v_in, v_ref),
                (out_in, out_tab), (inn_in, inn_tab), (back_in, back_tab),
                (last_in, last_tab), (turn_in, turn_tab),
            )
        )
    ]
    for copy in arrivals:
        copy.start()

    def z_copy(kind, src, dst, index):
        return pltpu.make_async_remote_copy(
            src_ref=src, dst_ref=dst, send_sem=z_send.at[kind], recv_sem=z_recv.at[kind],
            device_id=device(col, index), device_id_type=MESH,
        )

    def xy_copy(kind, src, dst, index):
        return pltpu.make_async_remote_copy(
            src_ref=src, dst_ref=dst, send_sem=xy_send.at[kind], recv_sem=xy_recv.at[kind],
            device_id=device(index, zc), device_id_type=MESH,
        )

    def far_copy(kind, src, dst, there, depth):
        return pltpu.make_async_remote_copy(
            src_ref=src, dst_ref=dst, send_sem=far_send.at[kind], recv_sem=far_recv.at[kind],
            device_id=device(there, depth), device_id_type=MESH,
        )

    def columns(index):
        return pl.ds(pl.multiple_of(index * BLOCK, BLOCK), BLOCK)

    def turned(block):
        return block.T.astype(BF16).reshape(DEPTH, OWN, BLOCK)

    arrivals[0].wait()

    def cut_filter(index, carry):
        cut_f[index] = turned(f_ref[:, columns(index)].astype(F32))
        return carry

    lax.fori_loop(0, COLS, cut_filter, 0)
    pl.semaphore_wait(barrier, 30)

    def announce(step, carry):
        target = device(beside(step), zc)
        pl.semaphore_signal(ready, inc=1, device_id=target, device_id_type=MESH)
        return carry

    lax.fori_loop(1, COLS, announce, 0)
    flip = lax.rem(col // 4 + col + core, 2)

    def send_filter(step, carry):
        turn = step // 2
        away = jnp.where(turn == 3, jnp.where(flip == 0, 2, 6), jnp.where(turn == 2, 7, turn))
        index = lax.rem(z + away, 8) * 2 + lax.rem(core + step, 2)
        z_copy(0, cut_f.at[:, index], mid_f.at[low], index).start()
        return carry

    lax.fori_loop(1, 8, send_filter, 0)
    own_f = pltpu.make_async_copy(cut_f.at[:, zc], mid_f.at[low], loc.at[0])
    own_f.start()

    def cut_block(kind, step, left, right, cut, got):
        there = beside(step)
        cols = columns(there)
        product = left[:, cols].astype(F32) * right[:, cols].astype(F32)
        cut[pl.ds(there * DEPTH, DEPTH)] = turned(product.astype(BF16).astype(F32))
        return there

    def send_block(kind, there, depths, cut, got):
        for depth in depths:
            far_copy(kind, cut.at[there * DEPTH + depth], got.at[me], there, depth).start()

    def cut_product(kind, left, right, cut, got, before):
        there = cut_block(kind, 0, left, right, cut, got)
        send_block(kind, there, depths[1:], cut, got)
        before()

        def one(step, carry):
            there = cut_block(kind, step, left, right, cut, got)
            send_block(kind, there, depths, cut, got)
            return carry

        lax.fori_loop(1, COLS, one, 0)
        own = pltpu.make_async_copy(cut.at[me], got.at[me], loc.at[kind + 1])
        own.start()
        return own

    def far_done(kind, got, own):
        own.wait()
        part = got.at[pl.ds(0, COLS * DEPTH - 1)]
        far_copy(kind, part, part, col, depths[1]).wait_recv()

    def z_done(kind, mid, count):
        part = mid.at[pl.ds(0, count)]
        z_copy(kind, part, part, depths[1]).wait_recv()

    def cross(kind, mid, got):
        def one(step, carry):
            index = beside(step)
            xy_copy(kind, mid.at[:, index], got.at[col], index).start()
            return carry

        lax.fori_loop(1, COLS, one, 0)
        own = pltpu.make_async_copy(mid.at[:, col], got.at[col], loc.at[kind + 3])
        own.start()
        return own

    def xy_done(kind, got, own):
        own.wait()
        part = got.at[pl.ds(0, COLS - 1)]
        xy_copy(kind, part, part, beside(1)).wait_recv()

    arrivals[1].wait()
    arrivals[2].wait()
    own_p = cut_product(0, q_ref, k_ref, cut_p, got_p, lambda: pl.semaphore_wait(ready, COLS - 1))
    own_f.wait()
    z_done(0, mid_f, 7)
    side_f = cross(0, mid_f, got_f)
    arrivals[3].wait()
    arrivals[4].wait()
    own_g = cut_product(1, g_ref, v_ref, cut_g, got_g, lambda: None)
    for copy in arrivals[5:]:
        copy.wait()

    cos, sin = turn_tab[0], turn_tab[1]
    cos2 = jnp.concatenate([cos, cos], axis=1)
    sin2 = jnp.concatenate([sin, sin], axis=1)

    def forward(sig, depth):
        first = mul(out_tab[0, :, :depth], sig) + mul(out_tab[1, :, :depth], sig)
        real, imag = first[:LONG], first[LONG:]
        tr = real * cos2 + imag * sin2
        ti = imag * cos2 - real * sin2
        rows = jnp.concatenate(
            [
                jnp.concatenate([tr[:, :BLOCK], ti[:, :BLOCK]], axis=1),
                jnp.concatenate([tr[:, BLOCK:], ti[:, BLOCK:]], axis=1),
            ],
            axis=0,
        )
        hi, lo = halves(rows)
        return mul(hi, inn_tab[0]) + mul(hi, inn_tab[1]) + mul(lo, inn_tab[0])

    def inverse(spec, rows):
        hi, lo = halves(spec)
        mixed = mul(hi, back_tab[0]) + mul(hi, back_tab[1]) + mul(lo, back_tab[0])
        real = jnp.concatenate([mixed[:LONG, :BLOCK], mixed[LONG:, :BLOCK]], axis=1)
        imag = jnp.concatenate([mixed[:LONG, BLOCK:], mixed[LONG:, BLOCK:]], axis=1)
        both = jnp.concatenate([real * cos2 - imag * sin2, real * sin2 + imag * cos2], axis=0)
        hi, lo = halves(both)
        total = (
            mul(last_tab[0, :rows], hi) + mul(last_tab[1, :rows], hi) + mul(last_tab[0, :rows], lo)
        )
        return total * (1.0 / PERIOD / BLOCK)

    def times(left, right, conjugate):
        lr, li = left[:, :BLOCK], left[:, BLOCK:]
        rr, ri = right[:, :BLOCK], right[:, BLOCK:]
        if conjugate:
            return jnp.concatenate([lr * rr + li * ri, lr * ri - li * rr], axis=1)
        return jnp.concatenate([lr * rr - li * ri, lr * ri + li * rr], axis=1)

    def load(base, jump):
        parts = [wide[pl.ds(base + n * jump, 8, stride=OWN), :] for n in range(COLS)]
        return jnp.concatenate(parts, axis=0).astype(BF16)

    def store(base, jump, value):
        for n in range(COLS):
            wide[pl.ds(base + n * jump, 8, stride=OWN), :] = value[n * 8 : n * 8 + 8]

    def load_pair(one):
        top = [load(one, BLOCK), load(one + 1, BLOCK)]
        bottom = [load(one + 64, BLOCK), load(one + 65, BLOCK)]
        return jnp.concatenate(
            [jnp.concatenate(top, axis=1), jnp.concatenate(bottom, axis=1)], axis=0
        )

    def store_pair(one, value):
        store(one, BLOCK, value[:BLOCK, :BLOCK])
        store(one + 1, BLOCK, value[:BLOCK, BLOCK:])
        store(one + 64, BLOCK, value[BLOCK:, :BLOCK])
        store(one + 65, BLOCK, value[BLOCK:, BLOCK:])

    def spread(got):
        value = got[...].astype(F32)
        rows = value.size // BLOCK
        wide[pl.ds(0, rows), :] = value.reshape(rows, BLOCK)

    def gather(out):
        rows = out.shape[0] * out.shape[1] * OWN
        out[...] = wide[pl.ds(0, rows), :].astype(BF16).reshape(out.shape)

    xy_done(0, got_f, side_f)
    spread(got_f)

    def filter_spectrum(pair, carry):
        one = 2 * pair
        sig = jnp.concatenate([load(one, 64), load(one + 1, 64)], axis=1)
        spec_h[pair] = forward(sig, BLOCK)
        return carry

    lax.fori_loop(0, OWN // 2, filter_spectrum, 0)

    far_done(0, got_p, own_p)
    spread(got_p)

    def convolve(pair, carry):
        spec = forward(load_pair(2 * pair), 2 * BLOCK)
        spec_p[pair] = spec
        store_pair(2 * pair, inverse(times(spec_h[pair], spec, False), 2 * BLOCK))
        return carry

    lax.fori_loop(0, OWN // 2, convolve, 0)
    gather(send_c)

    def deliver(kind, out, mid):
        def one(step, carry):
            index = around(step)
            z_copy(kind, out.at[:, index], mid.at[zc], index).start()
            return carry

        lax.fori_loop(1, DEPTH, one, 0)
        own = pltpu.make_async_copy(out.at[:, zc], mid.at[zc], loc.at[kind + 5])
        own.start()
        return own

    own_c = deliver(1, send_c, half_c)

    far_done(1, got_g, own_g)
    spread(got_g)

    def correlate(pair, carry):
        spec = forward(load_pair(2 * pair), 2 * BLOCK)
        store_pair(2 * pair, inverse(times(spec_h[pair], spec, True), 2 * BLOCK))
        spec_p[pair] = times(spec_p[pair], spec, True)
        return carry

    lax.fori_loop(0, OWN // 2, correlate, 0)
    gather(send_d)
    own_d = deliver(2, send_d, half_d)

    def lag(pair, carry):
        value = inverse(spec_p[pair], BLOCK)
        store(2 * pair, 64, value[:, :BLOCK])
        store(2 * pair + 1, 64, value[:, BLOCK:])
        return carry

    lax.fori_loop(0, OWN // 2, lag, 0)
    gather(send_l)

    def send_lag(there, depths):
        for depth in depths:
            far_copy(2, send_l.at[there, depth % 8], end_l.at[me], there, depth).start()

    def deliver_lag(step, carry):
        send_lag(beside(step), depths)
        return carry

    send_lag(col, depths[1:])
    lax.fori_loop(1, COLS, deliver_lag, 0)
    own_l = pltpu.make_async_copy(send_l.at[col, low], end_l.at[me], loc.at[8])
    own_l.start()

    own_c.wait()
    z_done(1, half_c, DEPTH - 1)
    side_c = cross(1, half_c, end_c)
    own_d.wait()
    z_done(2, half_d, DEPTH - 1)
    side_d = cross(2, half_d, end_d)

    def home(block):
        return block.astype(F32).reshape(BLOCK, BLOCK).T

    def finish_value(index, carry):
        cols = columns(index)
        dv_ref[:, cols] = (home(end_c[index]) * g_ref[:, cols].astype(F32)).astype(BF16)
        return carry

    xy_done(1, end_c, side_c)
    lax.fori_loop(0, COLS, finish_value, 0)
    away_v = pltpu.make_async_copy(dv_ref, dv_out, leave.at[0])
    away_v.start()

    def finish_gates(index, carry):
        cols = columns(index)
        back = home(end_d[index])
        dq_ref[:, cols] = (back * k_ref[:, cols].astype(F32)).astype(BF16)
        dk_ref[:, cols] = (back * q_ref[:, cols].astype(F32)).astype(BF16)
        return carry

    xy_done(2, end_d, side_d)
    lax.fori_loop(0, COLS, finish_gates, 0)
    away_q = pltpu.make_async_copy(dq_ref, dq_out, leave.at[1])
    away_q.start()
    away_k = pltpu.make_async_copy(dk_ref, dk_out, leave.at[2])
    away_k.start()

    def finish_filter(index, carry):
        block = end_l[pl.ds(index * DEPTH, DEPTH)]
        df_ref[:, columns(index)] = home(block).astype(BF16)
        return carry

    far_done(2, end_l, own_l)
    lax.fori_loop(0, COLS, finish_filter, 0)
    away_f = pltpu.make_async_copy(df_ref, df_out, leave.at[3])
    away_f.start()

    for kind in range(3):
        part = mid_f.at[pl.ds(0, 7)] if kind == 0 else half_c.at[pl.ds(0, DEPTH - 1)]
        z_copy(kind, part, part, depths[1]).wait_send()
        part = (got_f if kind == 0 else end_c).at[pl.ds(0, COLS - 1)]
        xy_copy(kind, part, part, beside(1)).wait_send()
        part = got_p.at[pl.ds(0, COLS * DEPTH - 1)]
        far_copy(kind, part, part, col, depths[1]).wait_send()
    for copy in (away_v, away_q, away_k, away_f):
        copy.wait()


def settle(*refs):
    sources, targets, stops, (into, onward) = refs[:4], refs[4:8], refs[8:12], refs[12:]
    arrivals = [pltpu.make_async_copy(sources[n], stops[n], into.at[n]) for n in range(4)]
    for copy in arrivals:
        copy.start()
    leaving = [pltpu.make_async_copy(stops[n], targets[n], onward.at[n]) for n in range(4)]
    for first, second in zip(arrivals, leaving, strict=True):
        first.wait()
        second.start()
    for copy in leaving:
        copy.wait()


def per_device(query_proj, key_proj, value_proj, out_grad, raw_filter):
    shape = jax.ShapeDtypeStruct(query_proj.shape, BF16)
    full = pltpu.VMEM((COLS, DEPTH, OWN, BLOCK), BF16)
    half = pltpu.VMEM((COLS, DEPTH // 2, OWN, BLOCK), BF16)
    near = pltpu.VMEM((DEPTH // 2, COLS, OWN, BLOCK), BF16)
    flat = pltpu.VMEM((COLS * DEPTH, OWN, BLOCK), BF16)
    consts = tuple(jnp.asarray(table) for table in tables())
    whole = pltpu.VMEM(query_proj.shape, BF16)
    spectra = pltpu.VMEM((OWN // 2, 2 * LONG, 2 * BLOCK), F32)
    anywhere = pl.BlockSpec(memory_space=pl.ANY)
    outs = pl.pallas_call(
        kernel,
        out_shape=(shape,) * 4,
        in_specs=[anywhere] * (5 + len(consts)),
        out_specs=(anywhere,) * 4,
        scratch_shapes=[
            *([whole] * 5),
            *(pltpu.VMEM(table.shape, table.dtype) for table in consts),
            *([whole] * 4),
            full, near, half, flat, flat, flat, flat,
            full, full, full, full, full, full, half, flat,
            pltpu.VMEM((COLS * DEPTH * OWN, BLOCK), F32),
            spectra, spectra,
            *([pltpu.SemaphoreType.DMA((3,))] * 6),
            pltpu.SemaphoreType.DMA((9,)),
            pltpu.SemaphoreType.DMA((10,)),
            pltpu.SemaphoreType.DMA((4,)),
            pltpu.SemaphoreType.REGULAR,
        ],
        compiler_params=pltpu.CompilerParams(
            collective_id=0, has_side_effects=True, vmem_limit_bytes=60 * 1024 * 1024
        ),
    )(query_proj, key_proj, value_proj, out_grad, raw_filter, *consts)
    return pl.pallas_call(
        settle,
        out_shape=(shape,) * 4,
        in_specs=[anywhere] * 4,
        out_specs=(anywhere,) * 4,
        scratch_shapes=[*([whole] * 4), *([pltpu.SemaphoreType.DMA((4,))] * 2)],
        compiler_params=pltpu.CompilerParams(vmem_limit_bytes=60 * 1024 * 1024),
    )(*outs)


def solution(mesh):
    in_specs = (P("ctx", "tp"), P("ctx", "tp"), P("ctx", "tp"), P("ctx", "tp"), P("ctx", None))
    out_specs = (P("ctx", "tp"), P("ctx", "tp"), P("ctx", "tp"), P("ctx", None))
    return jax.shard_map(
        per_device, mesh=mesh, in_specs=in_specs, out_specs=out_specs, check_vma=False
    )
```

time: 110 us -> 86.4 us (0.79)
  Pallas kernels: 103 us -> 85.7 us
  local copies, waits for them, and re-layouts: 5.19 us -> 0 us
    pallas_call x1 -> x2, Pallas kernels: 103 us -> 85.7 us  [the longest x1 83.2 us: per_device(): pl.pallas_call(kernel, out_shape=(shape,) * 4, in_specs=[anywhere] * (5 +...]
    unnamed x10 -> x0, local copies, waits for them, and re-layouts: 5.19 us -> none
where the time goes in v1:
time: 86.4 us; the launch traced here: 86.3 us
  Pallas kernels  85.7 us (99%)
    pallas_call x1, Pallas kernels, per_device(): pl.pallas_call(kernel, out_shape=(shape,) * 4, in_specs=[anywhere] * (5 +...  83.2 us
    pallas_call x1, Pallas kernels, per_device(): pl.pallas_call(settle, out_shape=(shape,) * 4, in_specs=[anywhere] * 4, o...  2.42 us

profile of v1, /device:TPU:1, one launch (start us, length us, event | category | flops | bytes accessed | tf_op | source)
XLA Modules:
  0.0 86.3 jit_solution(8090677647157314287)
XLA Ops:
  0.6 83.2 %shard_map.129 = (bf16[128,2048]{1,0:T(8,128)(2,1)}, bf16[128,2048]{1,0:T(8,128)(2,1)}, bf16[128,2048]{1,0:T(8,128)(2,1)}, bf16[128,2048]{1,0:T(8,128)(2,1)}) custom-call(bf16[128,2048]{1,0:T(8,128)(2,1)} %q_in.1, bf16[128,2048]{1,0:T(8,128)(2,1)} %k_in.1, bf16[128,2048]{1,0:T(8,128)(2,1)} %v_in.1, bf16[128,2048]{1,0:T(8,128)(2,1)} %g_in.1, ...), custom_call_target="tpu_custom_call" | custom-call | tf_op jit(solution)/shard_map/pallas_call | solution.py:437
  83.9 2.4 %shard_map.130 = (bf16[128,2048]{1,0:T(8,128)(2,1)}, bf16[128,2048]{1,0:T(8,128)(2,1)}, bf16[128,2048]{1,0:T(8,128)(2,1)}, bf16[128,2048]{1,0:T(8,128)(2,1)}) custom-call(bf16[128,2048]{1,0:T(8,128)(2,1)} %get-tuple-element.8.refs_0_, bf16[128,2048]{1,0:T(8,128)(2,1)} %get-tuple-element.9.refs_1_, bf16[128,2048]{1,0:T(8,128)(2,1)} %get-tuple-element.10.refs_2_, ...), custom_call_target="tpu_custom_call" | custom-call | tf_op jit(solution)/shard_map/pallas_call | solution.py:460

commit v2 on v1

--- a/solution.py
+++ b/solution.py
@@ -53,13 +53,12 @@
 
 def kernel(
     q_in, k_in, v_in, g_in, f_in, out_in, inn_in, back_in, last_in, turn_in,
-    dq_out, dk_out, dv_out, df_out,
+    dq_ref, dk_ref, dv_ref, df_ref,
     q_ref, k_ref, v_ref, g_ref, f_ref, out_tab, inn_tab, back_tab, last_tab, turn_tab,
-    dq_ref, dk_ref, dv_ref, df_ref,
     cut_f, mid_f, got_f, cut_p, got_p, cut_g, got_g,
-    send_c, half_c, end_c, send_d, half_d, end_d, send_l, end_l,
+    send_c, half_c, end_c, send_d, end_d, send_l, end_l,
     wide, spec_h, spec_p,
-    z_send, z_recv, xy_send, xy_recv, far_send, far_recv, loc, fetch, leave, ready,
+    z_send, z_recv, xy_send, xy_recv, far_send, far_recv, loc, fetch, ready,
 ):
     ctx, tp = lax.axis_index("ctx"), lax.axis_index("tp")
     col = ctx // 8
@@ -294,7 +293,7 @@
         spec_h[pair] = forward(sig, BLOCK)
         return carry
 
-    lax.fori_loop(0, OWN // 2, filter_spectrum, 0)
+    lax.fori_loop(0, OWN // 2, filter_spectrum, 0, unroll=2)
 
     far_done(0, got_p, own_p)
     spread(got_p)
@@ -305,7 +304,7 @@
         store_pair(2 * pair, inverse(times(spec_h[pair], spec, False), 2 * BLOCK))
         return carry
 
-    lax.fori_loop(0, OWN // 2, convolve, 0)
+    lax.fori_loop(0, OWN // 2, convolve, 0, unroll=2)
     gather(send_c)
 
     def deliver(kind, out, mid):
@@ -330,9 +329,26 @@
         spec_p[pair] = times(spec_p[pair], spec, True)
         return carry
 
-    lax.fori_loop(0, OWN // 2, correlate, 0)
+    lax.fori_loop(0, OWN // 2, correlate, 0, unroll=2)
     gather(send_d)
-    own_d = deliver(2, send_d, half_d)
+
+    def deliver_far(kind, out, end):
+        def send(there, depths):
+            for depth in depths:
+                src = out.at[there, depth % out.shape[1]]
+                far_copy(kind, src, end.at[me], there, depth).start()
+
+        def one(step, carry):
+            send(beside(step), depths)
+            return carry
+
+        send(col, depths[1:])
+        lax.fori_loop(1, COLS, one, 0)
+        own = pltpu.make_async_copy(out.at[col, lax.rem(zc, out.shape[1])], end.at[me], loc.at[kind + 5])
+        own.start()
+        return own
+
+    own_d = deliver_far(2, send_d, end_d)
 
     def lag(pair, carry):
         value = inverse(spec_p[pair], BLOCK)
@@ -340,28 +356,14 @@
         store(2 * pair + 1, 64, value[:, BLOCK:])
         return carry
 
-    lax.fori_loop(0, OWN // 2, lag, 0)
+    lax.fori_loop(0, OWN // 2, lag, 0, unroll=2)
     gather(send_l)
 
-    def send_lag(there, depths):
-        for depth in depths:
-            far_copy(2, send_l.at[there, depth % 8], end_l.at[me], there, depth).start()
-
-    def deliver_lag(step, carry):
-        send_lag(beside(step), depths)
-        return carry
-
-    send_lag(col, depths[1:])
-    lax.fori_loop(1, COLS, deliver_lag, 0)
-    own_l = pltpu.make_async_copy(send_l.at[col, low], end_l.at[me], loc.at[8])
-    own_l.start()
+    own_l = deliver_far(3, send_l, end_l)
 
     own_c.wait()
     z_done(1, half_c, DEPTH - 1)
     side_c = cross(1, half_c, end_c)
-    own_d.wait()
-    z_done(2, half_d, DEPTH - 1)
-    side_d = cross(2, half_d, end_d)
 
     def home(block):
         return block.astype(F32).reshape(BLOCK, BLOCK).T
@@ -371,56 +373,41 @@
         dv_ref[:, cols] = (home(end_c[index]) * g_ref[:, cols].astype(F32)).astype(BF16)
         return carry
 
+    def finish_gates(index, carry):
+        cols = columns(index)
+        back = home(end_d[pl.ds(index * DEPTH, DEPTH)])
+        dq_ref[:, cols] = (back * k_ref[:, cols].astype(F32)).astype(BF16)
+        dk_ref[:, cols] = (back * q_ref[:, cols].astype(F32)).astype(BF16)
+        return carry
+
     xy_done(1, end_c, side_c)
     lax.fori_loop(0, COLS, finish_value, 0)
-    away_v = pltpu.make_async_copy(dv_ref, dv_out, leave.at[0])
-    away_v.start()
-
-    def finish_gates(index, carry):
-        cols = columns(index)
-        back = home(end_d[index])
-        dq_ref[:, cols] = (back * k_ref[:, cols].astype(F32)).astype(BF16)
-        dk_ref[:, cols] = (back * q_ref[:, cols].astype(F32)).astype(BF16)
-        return carry
-
-    xy_done(2, end_d, side_d)
+    far_done(2, end_d, own_d)
     lax.fori_loop(0, COLS, finish_gates, 0)
-    away_q = pltpu.make_async_copy(dq_ref, dq_out, leave.at[1])
-    away_q.start()
-    away_k = pltpu.make_async_copy(dk_ref, dk_out, leave.at[2])
-    away_k.start()
 
     def finish_filter(index, carry):
         block = end_l[pl.ds(index * DEPTH, DEPTH)]
         df_ref[:, columns(index)] = home(block).astype(BF16)
         return carry
 
-    far_done(2, end_l, own_l)
+    far_done(3, end_l, own_l)
     lax.fori_loop(0, COLS, finish_filter, 0)
-    away_f = pltpu.make_async_copy(df_ref, df_out, leave.at[3])
-    away_f.start()
-
-    for kind in range(3):
+
+    for kind in range(2):
         part = mid_f.at[pl.ds(0, 7)] if kind == 0 else half_c.at[pl.ds(0, DEPTH - 1)]
         z_copy(kind, part, part, depths[1]).wait_send()
         part = (got_f if kind == 0 else end_c).at[pl.ds(0, COLS - 1)]
         xy_copy(kind, part, part, beside(1)).wait_send()
+    for kind in range(4):
         part = got_p.at[pl.ds(0, COLS * DEPTH - 1)]
         far_copy(kind, part, part, col, depths[1]).wait_send()
-    for copy in (away_v, away_q, away_k, away_f):
-        copy.wait()
 
 
 def settle(*refs):
-    sources, targets, stops, (into, onward) = refs[:4], refs[4:8], refs[8:12], refs[12:]
-    arrivals = [pltpu.make_async_copy(sources[n], stops[n], into.at[n]) for n in range(4)]
-    for copy in arrivals:
+    copies = [pltpu.make_async_copy(refs[n], refs[n + 4], refs[8].at[n]) for n in range(4)]
+    for copy in copies:
         copy.start()
-    leaving = [pltpu.make_async_copy(stops[n], targets[n], onward.at[n]) for n in range(4)]
-    for first, second in zip(arrivals, leaving, strict=True):
-        first.wait()
-        second.start()
-    for copy in leaving:
+    for copy in copies:
         copy.wait()
 
 
@@ -436,25 +423,24 @@
     anywhere = pl.BlockSpec(memory_space=pl.ANY)
     outs = pl.pallas_call(
         kernel,
-        out_shape=(shape,) * 4,
+        out_shape=(pltpu.VMEM(query_proj.shape, BF16),) * 4,
         in_specs=[anywhere] * (5 + len(consts)),
-        out_specs=(anywhere,) * 4,
+        out_specs=(pl.BlockSpec(memory_space=pltpu.VMEM),) * 4,
         scratch_shapes=[
             *([whole] * 5),
             *(pltpu.VMEM(table.shape, table.dtype) for table in consts),
-            *([whole] * 4),
             full, near, half, flat, flat, flat, flat,
-            full, full, full, full, full, full, half, flat,
+            full, full, full, full, flat, half, flat,
             pltpu.VMEM((COLS * DEPTH * OWN, BLOCK), F32),
             spectra, spectra,
-            *([pltpu.SemaphoreType.DMA((3,))] * 6),
+            *([pltpu.SemaphoreType.DMA((2,))] * 4),
+            *([pltpu.SemaphoreType.DMA((4,))] * 2),
             pltpu.SemaphoreType.DMA((9,)),
             pltpu.SemaphoreType.DMA((10,)),
-            pltpu.SemaphoreType.DMA((4,)),
             pltpu.SemaphoreType.REGULAR,
         ],
         compiler_params=pltpu.CompilerParams(
-            collective_id=0, has_side_effects=True, vmem_limit_bytes=60 * 1024 * 1024
+            collective_id=0, has_side_effects=True, vmem_limit_bytes=58 * 1024 * 1024
         ),
     )(query_proj, key_proj, value_proj, out_grad, raw_filter, *consts)
     return pl.pallas_call(
@@ -462,8 +448,8 @@
         out_shape=(shape,) * 4,
         in_specs=[anywhere] * 4,
         out_specs=(anywhere,) * 4,
-        scratch_shapes=[*([whole] * 4), *([pltpu.SemaphoreType.DMA((4,))] * 2)],
-        compiler_params=pltpu.CompilerParams(vmem_limit_bytes=60 * 1024 * 1024),
+        scratch_shapes=[pltpu.SemaphoreType.DMA((4,))],
+        compiler_params=pltpu.CompilerParams(vmem_limit_bytes=1024 * 1024),
     )(*outs)
 
 

time: 86.4 us -> 79.5 us (0.920)
  Pallas kernels: 85.7 us -> 78.8 us
    pallas_call x1, Pallas kernels: 83.2 us -> 77.5 us  [per_device(): pl.pallas_call(kernel, out_shape=(pltpu.VMEM(query_proj.shape, BF16),) *...]
    pallas_call x1, Pallas kernels: 2.42 us -> 1.35 us  [per_device(): pl.pallas_call(settle, out_shape=(shape,) * 4, in_specs=[anywhere] * 4, o...]
where the time goes in v2:
time: 79.5 us; the launch traced here: 79.4 us
  Pallas kernels  78.8 us (99%)
    pallas_call x1, Pallas kernels, per_device(): pl.pallas_call(kernel, out_shape=(pltpu.VMEM(query_proj.shape, BF16),) *...  77.5 us

profile of v2, /device:TPU:1, one launch (start us, length us, event | category | flops | bytes accessed | tf_op | source)
XLA Modules:
  0.0 79.4 jit_solution(1084805922998855553)
XLA Ops:
  0.6 77.5 %shard_map.129 = (bf16[128,2048]{1,0:T(8,128)(2,1)S(1)}, bf16[128,2048]{1,0:T(8,128)(2,1)S(1)}, bf16[128,2048]{1,0:T(8,128)(2,1)S(1)}, bf16[128,2048]{1,0:T(8,128)(2,1)S(1)}) custom-call(bf16[128,2048]{1,0:T(8,128)(2,1)} %q_in.1, bf16[128,2048]{1,0:T(8,128)(2,1)} %k_in.1, bf16[128,2048]{1,0:T(8,128)(2,1)} %v_in.1, bf16[128,2048]{1,0:T(8,128)(2,1)} %g_in.1, ...), custom_call_target="tpu_custom_call" | custom-call | tf_op jit(solution)/shard_map/pallas_call | solution.py:424
  78.1 1.3 %shard_map.130 = (bf16[128,2048]{1,0:T(8,128)(2,1)}, bf16[128,2048]{1,0:T(8,128)(2,1)}, bf16[128,2048]{1,0:T(8,128)(2,1)}, bf16[128,2048]{1,0:T(8,128)(2,1)}) custom-call(bf16[128,2048]{1,0:T(8,128)(2,1)S(1)} %get-tuple-element.8.refs_0_, bf16[128,2048]{1,0:T(8,128)(2,1)S(1)} %get-tuple-element.9.refs_1_, bf16[128,2048]{1,0:T(8,128)(2,1)S(1)} %get-tuple-element.10.refs_2_, ...), custom_call_target="tpu_custom_call" | custom-call | tf_op jit(solution)/shard_map/pallas_call | solution.py:446

commit v3 on v2

--- a/solution.py
+++ b/solution.py
@@ -56,7 +56,7 @@
     dq_ref, dk_ref, dv_ref, df_ref,
     q_ref, k_ref, v_ref, g_ref, f_ref, out_tab, inn_tab, back_tab, last_tab, turn_tab,
     cut_f, mid_f, got_f, cut_p, got_p, cut_g, got_g,
-    send_c, half_c, end_c, send_d, end_d, send_l, end_l,
+    send_c, end_c, send_d, end_d, send_l, end_l,
     wide, spec_h, spec_p,
     z_send, z_recv, xy_send, xy_recv, far_send, far_recv, loc, fetch, ready,
 ):
@@ -78,15 +78,22 @@
         along = lax.rem(col // 4 + step // 4, 4)
         return along * 4 + across
 
-    depths = [around(step) for step in range(DEPTH)]
+    def distant(step):
+        along, across = 3 - step // 4, 3 - step % 4
+        turns = [jnp.where(n == 2, 3, jnp.where(n == 3, 2, n)) for n in (along, across)]
+        return turns[0] * 4 + turns[1]
+
+    hops = (8, 9, 6, 11, 7, 10, 4, 13, 5, 12, 2, 15, 3, 14, 1)
+    depths = [around(step) for step in hops]
+    everyone = [*depths, zc]
     barrier = pltpu.get_barrier_semaphore()
 
-    def greet(step, carry):
-        for target in (device(col, around(step)), device(beside(step), zc)):
-            pl.semaphore_signal(barrier, inc=1, device_id=target, device_id_type=MESH)
-        return carry
-
-    lax.fori_loop(1, 16, greet, 0)
+    def greet(target):
+        pl.semaphore_signal(barrier, inc=1, device_id=target, device_id_type=MESH)
+
+    for step, depth in enumerate(depths):
+        greet(device(col, depth))
+        greet(device(beside(distant(step)), zc))
 
     arrivals = [
         pltpu.make_async_copy(src, dst, fetch.at[n])
@@ -113,9 +120,9 @@
             device_id=device(index, zc), device_id_type=MESH,
         )
 
-    def far_copy(kind, src, dst, there, depth):
+    def far_copy(kind, src, dst, there, depth, part=0):
         return pltpu.make_async_remote_copy(
-            src_ref=src, dst_ref=dst, send_sem=far_send.at[kind], recv_sem=far_recv.at[kind],
+            src_ref=src, dst_ref=dst, send_sem=far_send.at[kind], recv_sem=far_recv.at[kind + part],
             device_id=device(there, depth), device_id_type=MESH,
         )
 
@@ -134,12 +141,9 @@
     lax.fori_loop(0, COLS, cut_filter, 0)
     pl.semaphore_wait(barrier, 30)
 
-    def announce(step, carry):
-        target = device(beside(step), zc)
+    for step in range(COLS - 1):
+        target = device(beside(distant(step)), zc)
         pl.semaphore_signal(ready, inc=1, device_id=target, device_id_type=MESH)
-        return carry
-
-    lax.fori_loop(1, COLS, announce, 0)
     flip = lax.rem(col // 4 + col + core, 2)
 
     def send_filter(step, carry):
@@ -149,32 +153,29 @@
         z_copy(0, cut_f.at[:, index], mid_f.at[low], index).start()
         return carry
 
-    lax.fori_loop(1, 8, send_filter, 0)
+    lax.fori_loop(0, 7, lambda n, carry: send_filter(7 - n, carry), 0)
     own_f = pltpu.make_async_copy(cut_f.at[:, zc], mid_f.at[low], loc.at[0])
     own_f.start()
 
-    def cut_block(kind, step, left, right, cut, got):
-        there = beside(step)
-        cols = columns(there)
-        product = left[:, cols].astype(F32) * right[:, cols].astype(F32)
-        cut[pl.ds(there * DEPTH, DEPTH)] = turned(product.astype(BF16).astype(F32))
-        return there
+    def cut_product(left, right, cut):
+        def one(there, carry):
+            cols = columns(there)
+            product = left[:, cols].astype(F32) * right[:, cols].astype(F32)
+            cut[pl.ds(there * DEPTH, DEPTH)] = turned(product.astype(BF16).astype(F32))
+            return carry
+
+        lax.fori_loop(0, COLS, one, 0)
 
     def send_block(kind, there, depths, cut, got):
         for depth in depths:
             far_copy(kind, cut.at[there * DEPTH + depth], got.at[me], there, depth).start()
 
-    def cut_product(kind, left, right, cut, got, before):
-        there = cut_block(kind, 0, left, right, cut, got)
-        send_block(kind, there, depths[1:], cut, got)
-        before()
-
+    def send_product(kind, cut, got):
         def one(step, carry):
-            there = cut_block(kind, step, left, right, cut, got)
-            send_block(kind, there, depths, cut, got)
+            send_block(kind, beside(distant(step)), everyone, cut, got)
             return carry
 
-        lax.fori_loop(1, COLS, one, 0)
+        lax.fori_loop(0, COLS - 1, one, 0)
         own = pltpu.make_async_copy(cut.at[me], got.at[me], loc.at[kind + 1])
         own.start()
         return own
@@ -182,37 +183,42 @@
     def far_done(kind, got, own):
         own.wait()
         part = got.at[pl.ds(0, COLS * DEPTH - 1)]
-        far_copy(kind, part, part, col, depths[1]).wait_recv()
+        far_copy(kind, part, part, col, depths[0]).wait_recv()
 
     def z_done(kind, mid, count):
         part = mid.at[pl.ds(0, count)]
-        z_copy(kind, part, part, depths[1]).wait_recv()
+        z_copy(kind, part, part, depths[0]).wait_recv()
 
     def cross(kind, mid, got):
         def one(step, carry):
-            index = beside(step)
+            index = beside(distant(step))
             xy_copy(kind, mid.at[:, index], got.at[col], index).start()
             return carry
 
-        lax.fori_loop(1, COLS, one, 0)
-        own = pltpu.make_async_copy(mid.at[:, col], got.at[col], loc.at[kind + 3])
+        lax.fori_loop(0, COLS - 1, one, 0)
+        own = pltpu.make_async_copy(mid.at[:, col], got.at[col], loc.at[7])
         own.start()
         return own
 
     def xy_done(kind, got, own):
         own.wait()
         part = got.at[pl.ds(0, COLS - 1)]
-        xy_copy(kind, part, part, beside(1)).wait_recv()
+        xy_copy(kind, part, part, beside(distant(0))).wait_recv()
 
     arrivals[1].wait()
     arrivals[2].wait()
-    own_p = cut_product(0, q_ref, k_ref, cut_p, got_p, lambda: pl.semaphore_wait(ready, COLS - 1))
+    cut_product(q_ref, k_ref, cut_p)
+    send_block(0, col, depths, cut_p, got_p)
+    arrivals[3].wait()
+    arrivals[4].wait()
+    cut_product(g_ref, v_ref, cut_g)
+    pl.semaphore_wait(ready, COLS - 1)
+    own_p = send_product(0, cut_p, got_p)
     own_f.wait()
     z_done(0, mid_f, 7)
     side_f = cross(0, mid_f, got_f)
-    arrivals[3].wait()
-    arrivals[4].wait()
-    own_g = cut_product(1, g_ref, v_ref, cut_g, got_g, lambda: None)
+    own_g = send_product(1, cut_g, got_g)
+    send_block(1, col, depths, cut_g, got_g)
     for copy in arrivals[5:]:
         copy.wait()
 
@@ -293,7 +299,7 @@
         spec_h[pair] = forward(sig, BLOCK)
         return carry
 
-    lax.fori_loop(0, OWN // 2, filter_spectrum, 0, unroll=2)
+    lax.fori_loop(0, OWN // 2, filter_spectrum, 0, unroll=4)
 
     far_done(0, got_p, own_p)
     spread(got_p)
@@ -304,21 +310,26 @@
         store_pair(2 * pair, inverse(times(spec_h[pair], spec, False), 2 * BLOCK))
         return carry
 
-    lax.fori_loop(0, OWN // 2, convolve, 0, unroll=2)
+    lax.fori_loop(0, OWN // 2, convolve, 0, unroll=4)
     gather(send_c)
 
-    def deliver(kind, out, mid):
+    def deliver_far(kind, out, end):
+        def send(there, depths, part):
+            for depth in depths:
+                src = out.at[there, depth % out.shape[1]]
+                far_copy(kind, src, end.at[me], there, depth, part).start()
+
         def one(step, carry):
-            index = around(step)
-            z_copy(kind, out.at[:, index], mid.at[zc], index).start()
+            send(beside(distant(step)), everyone, step // 4 if kind == 4 else 0)
             return carry
 
-        lax.fori_loop(1, DEPTH, one, 0)
-        own = pltpu.make_async_copy(out.at[:, zc], mid.at[zc], loc.at[kind + 5])
+        lax.fori_loop(0, COLS - 1, one, 0)
+        send(col, depths, 3 if kind == 4 else 0)
+        own = pltpu.make_async_copy(out.at[col, lax.rem(zc, out.shape[1])], end.at[me], loc.at[kind + 2])
         own.start()
         return own
 
-    own_c = deliver(1, send_c, half_c)
+    own_c = deliver_far(2, send_c, end_c)
 
     far_done(1, got_g, own_g)
     spread(got_g)
@@ -329,26 +340,10 @@
         spec_p[pair] = times(spec_p[pair], spec, True)
         return carry
 
-    lax.fori_loop(0, OWN // 2, correlate, 0, unroll=2)
+    lax.fori_loop(0, OWN // 2, correlate, 0, unroll=4)
     gather(send_d)
 
-    def deliver_far(kind, out, end):
-        def send(there, depths):
-            for depth in depths:
-                src = out.at[there, depth % out.shape[1]]
-                far_copy(kind, src, end.at[me], there, depth).start()
-
-        def one(step, carry):
-            send(beside(step), depths)
-            return carry
-
-        send(col, depths[1:])
-        lax.fori_loop(1, COLS, one, 0)
-        own = pltpu.make_async_copy(out.at[col, lax.rem(zc, out.shape[1])], end.at[me], loc.at[kind + 5])
-        own.start()
-        return own
-
-    own_d = deliver_far(2, send_d, end_d)
+    own_d = deliver_far(3, send_d, end_d)
 
     def lag(pair, carry):
         value = inverse(spec_p[pair], BLOCK)
@@ -356,21 +351,17 @@
         store(2 * pair + 1, 64, value[:, BLOCK:])
         return carry
 
-    lax.fori_loop(0, OWN // 2, lag, 0, unroll=2)
+    lax.fori_loop(0, OWN // 2, lag, 0, unroll=4)
     gather(send_l)
 
-    own_l = deliver_far(3, send_l, end_l)
-
-    own_c.wait()
-    z_done(1, half_c, DEPTH - 1)
-    side_c = cross(1, half_c, end_c)
+    own_l = deliver_far(4, send_l, end_l)
 
     def home(block):
         return block.astype(F32).reshape(BLOCK, BLOCK).T
 
     def finish_value(index, carry):
         cols = columns(index)
-        dv_ref[:, cols] = (home(end_c[index]) * g_ref[:, cols].astype(F32)).astype(BF16)
+        dv_ref[:, cols] = (home(end_c[pl.ds(index * DEPTH, DEPTH)]) * g_ref[:, cols].astype(F32)).astype(BF16)
         return carry
 
     def finish_gates(index, carry):
@@ -380,9 +371,9 @@
         dk_ref[:, cols] = (back * q_ref[:, cols].astype(F32)).astype(BF16)
         return carry
 
-    xy_done(1, end_c, side_c)
+    far_done(2, end_c, own_c)
     lax.fori_loop(0, COLS, finish_value, 0)
-    far_done(2, end_d, own_d)
+    far_done(3, end_d, own_d)
     lax.fori_loop(0, COLS, finish_gates, 0)
 
     def finish_filter(index, carry):
@@ -390,17 +381,21 @@
         df_ref[:, columns(index)] = home(block).astype(BF16)
         return carry
 
-    far_done(3, end_l, own_l)
-    lax.fori_loop(0, COLS, finish_filter, 0)
-
-    for kind in range(2):
-        part = mid_f.at[pl.ds(0, 7)] if kind == 0 else half_c.at[pl.ds(0, DEPTH - 1)]
-        z_copy(kind, part, part, depths[1]).wait_send()
-        part = (got_f if kind == 0 else end_c).at[pl.ds(0, COLS - 1)]
-        xy_copy(kind, part, part, beside(1)).wait_send()
-    for kind in range(4):
+    own_l.wait()
+    for part in range(4):
+        some = end_l.at[pl.ds(0, 4 * DEPTH - (part == 3))]
+        far_copy(4, some, some, col, depths[0], part).wait_recv()
+        row = lax.rem(col // 4 + 4 - distant(4 * part) // 4, 4)
+        for n in range(4):
+            finish_filter(row * 4 + n, 0)
+
+    part = mid_f.at[pl.ds(0, 7)]
+    z_copy(0, part, part, depths[0]).wait_send()
+    part = got_f.at[pl.ds(0, COLS - 1)]
+    xy_copy(0, part, part, beside(distant(0))).wait_send()
+    for kind in range(5):
         part = got_p.at[pl.ds(0, COLS * DEPTH - 1)]
-        far_copy(kind, part, part, col, depths[1]).wait_send()
+        far_copy(kind, part, part, col, depths[0]).wait_send()
 
 
 def settle(*refs):
@@ -430,12 +425,13 @@
             *([whole] * 5),
             *(pltpu.VMEM(table.shape, table.dtype) for table in consts),
             full, near, half, flat, flat, flat, flat,
-            full, full, full, full, flat, half, flat,
+            full, flat, full, flat, half, flat,
             pltpu.VMEM((COLS * DEPTH * OWN, BLOCK), F32),
             spectra, spectra,
-            *([pltpu.SemaphoreType.DMA((2,))] * 4),
-            *([pltpu.SemaphoreType.DMA((4,))] * 2),
-            pltpu.SemaphoreType.DMA((9,)),
+            *([pltpu.SemaphoreType.DMA((1,))] * 4),
+            pltpu.SemaphoreType.DMA((5,)),
+            pltpu.SemaphoreType.DMA((8,)),
+            pltpu.SemaphoreType.DMA((8,)),
             pltpu.SemaphoreType.DMA((10,)),
             pltpu.SemaphoreType.REGULAR,
         ],

time: 79.5 us -> 75.9 us (0.955)
  Pallas kernels: 78.8 us -> 75 us
    pallas_call x1, Pallas kernels: 77.5 us -> 73.6 us  [per_device(): pl.pallas_call(kernel, out_shape=(pltpu.VMEM(query_proj.shape, BF16),) *...]
where the time goes in v3:
time: 75.9 us; the launch traced here: 75.8 us
  Pallas kernels  75 us (99%)
  between operations  0.8 us (1%)
    pallas_call x1, Pallas kernels, per_device(): pl.pallas_call(kernel, out_shape=(pltpu.VMEM(query_proj.shape, BF16),) *...  73.6 us

profile of v3, /device:TPU:1, one launch (start us, length us, event | category | flops | bytes accessed | tf_op | source)
XLA Modules:
  0.0 75.8 jit_solution(12272917118929961301)
XLA Ops:
  0.6 73.6 %shard_map.129 = (bf16[128,2048]{1,0:T(8,128)(2,1)S(1)}, bf16[128,2048]{1,0:T(8,128)(2,1)S(1)}, bf16[128,2048]{1,0:T(8,128)(2,1)S(1)}, bf16[128,2048]{1,0:T(8,128)(2,1)S(1)}) custom-call(bf16[128,2048]{1,0:T(8,128)(2,1)} %q_in.1, bf16[128,2048]{1,0:T(8,128)(2,1)} %k_in.1, bf16[128,2048]{1,0:T(8,128)(2,1)} %v_in.1, bf16[128,2048]{1,0:T(8,128)(2,1)} %g_in.1, ...), custom_call_target="tpu_custom_call" | custom-call | tf_op jit(solution)/shard_map/pallas_call | solution.py:419
  74.3 1.3 %shard_map.130 = (bf16[128,2048]{1,0:T(8,128)(2,1)}, bf16[128,2048]{1,0:T(8,128)(2,1)}, bf16[128,2048]{1,0:T(8,128)(2,1)}, bf16[128,2048]{1,0:T(8,128)(2,1)}) custom-call(bf16[128,2048]{1,0:T(8,128)(2,1)S(1)} %get-tuple-element.8.refs_0_, bf16[128,2048]{1,0:T(8,128)(2,1)S(1)} %get-tuple-element.9.refs_1_, bf16[128,2048]{1,0:T(8,128)(2,1)S(1)} %get-tuple-element.10.refs_2_, ...), custom_call_target="tpu_custom_call" | custom-call | tf_op jit(solution)/shard_map/pallas_call | solution.py:442

commit v4 on v3

--- a/solution.py
+++ b/solution.py
@@ -83,7 +83,7 @@
         turns = [jnp.where(n == 2, 3, jnp.where(n == 3, 2, n)) for n in (along, across)]
         return turns[0] * 4 + turns[1]
 
-    hops = (8, 9, 6, 11, 7, 10, 4, 13, 5, 12, 2, 15, 3, 14, 1)
+    hops = (8, 2, 14, 6, 10, 4, 12, 9, 3, 15, 7, 11, 5, 13, 1)
     depths = [around(step) for step in hops]
     everyone = [*depths, zc]
     barrier = pltpu.get_barrier_semaphore()
@@ -209,11 +209,11 @@
     arrivals[2].wait()
     cut_product(q_ref, k_ref, cut_p)
     send_block(0, col, depths, cut_p, got_p)
+    pl.semaphore_wait(ready, COLS - 1)
+    own_p = send_product(0, cut_p, got_p)
     arrivals[3].wait()
     arrivals[4].wait()
     cut_product(g_ref, v_ref, cut_g)
-    pl.semaphore_wait(ready, COLS - 1)
-    own_p = send_product(0, cut_p, got_p)
     own_f.wait()
     z_done(0, mid_f, 7)
     side_f = cross(0, mid_f, got_f)
@@ -426,7 +426,7 @@
             *(pltpu.VMEM(table.shape, table.dtype) for table in consts),
             full, near, half, flat, flat, flat, flat,
             full, flat, full, flat, half, flat,
-            pltpu.VMEM((COLS * DEPTH * OWN, BLOCK), F32),
+            pltpu.VMEM((COLS * DEPTH * OWN + 8 * OWN, BLOCK), F32),
             spectra, spectra,
             *([pltpu.SemaphoreType.DMA((1,))] * 4),
             pltpu.SemaphoreType.DMA((5,)),

time: 75.9 us -> 75.8 us (level)
  no operation moved by 1% of the time
where the time goes in v4:
time: 75.8 us
  Pallas kernels  75 us (99%)
  between operations  0.8 us (1%)
    pallas_call x1, Pallas kernels, per_device(): pl.pallas_call(kernel, out_shape=(pltpu.VMEM(query_proj.shape, BF16),) *...  73.6 us

profile of v4, /device:TPU:1, one launch (start us, length us, event | category | flops | bytes accessed | tf_op | source)
XLA Modules:
  0.0 75.8 jit_solution(17241766342302833646)
XLA Ops:
  0.6 73.6 %shard_map.129 = (bf16[128,2048]{1,0:T(8,128)(2,1)S(1)}, bf16[128,2048]{1,0:T(8,128)(2,1)S(1)}, bf16[128,2048]{1,0:T(8,128)(2,1)S(1)}, bf16[128,2048]{1,0:T(8,128)(2,1)S(1)}) custom-call(bf16[128,2048]{1,0:T(8,128)(2,1)} %q_in.1, bf16[128,2048]{1,0:T(8,128)(2,1)} %k_in.1, bf16[128,2048]{1,0:T(8,128)(2,1)} %v_in.1, bf16[128,2048]{1,0:T(8,128)(2,1)} %g_in.1, ...), custom_call_target="tpu_custom_call" | custom-call | tf_op jit(solution)/shard_map/pallas_call | solution.py:419
  74.3 1.3 %shard_map.130 = (bf16[128,2048]{1,0:T(8,128)(2,1)}, bf16[128,2048]{1,0:T(8,128)(2,1)}, bf16[128,2048]{1,0:T(8,128)(2,1)}, bf16[128,2048]{1,0:T(8,128)(2,1)}) custom-call(bf16[128,2048]{1,0:T(8,128)(2,1)S(1)} %get-tuple-element.8.refs_0_, bf16[128,2048]{1,0:T(8,128)(2,1)S(1)} %get-tuple-element.9.refs_1_, bf16[128,2048]{1,0:T(8,128)(2,1)S(1)} %get-tuple-element.10.refs_2_, ...), custom_call_target="tpu_custom_call" | custom-call | tf_op jit(solution)/shard_map/pallas_call | solution.py:442
